TPU v7x, 32 devices: a whole 2x2x4 slice. The times are simulated.
32 devices in a mesh: row: 4 (over y, x), col: 8 (over z, core).
Axes of the slice: x: 2, y: 2, z: 4, core: 2. Of those that a mesh axis runs over, the one named last changes fastest.
Arguments:
- tiles: bfloat16 [4, 8, 32, 128, 128], P('row', 'col'), may hold values from -0.5 to 0.5
- tile_slots: int32 [4, 8, 32], P('row', 'col'), may hold values from 0 to 191, as said below
- tile_counts: int32 [4, 8], P('row', 'col'), may hold values from 8 to 32, as said below
- user_degree: int32 [8192], P('row'), may hold values from 1 to 64
- item_degree: int32 [12288], P('col'), may hold values from 1 to 64
- start_panel: float32 [64, 12288], P(None, ('col', 'row')), may hold values from -6 to 6
Outputs:
- left_panel: float32 [64, 8192], P(None, ('row', 'col'))
- right_panel: float32 [64, 12288], P(None, ('col', 'row'))
- left_factors: float32 [3, 64, 64], replicated
- right_factors: float32 [3, 64, 64], replicated
Inputs may be any that keep to these rules, and one draw needn't show every extreme that they name: `tile_slots`: within one grid cell the 32 slot numbers are distinct; slot s is local tile row s // 12 and local tile column s % 12; entries from position tile_counts on are padding. `tile_counts`: some grid cell holds 32 live tiles.
All inputs are finite; a program needn't handle non-finite values.
Results may differ from a plain program's by a relative error of at most 0.0005.
Values sent between devices are 32-bit elements; how exact they have to be, the bound alone decides.
A program may use at most 64 MiB of HBM per device.

v0:
```python
import math

import jax
import jax.numpy as jnp
from jax import lax
from jax.sharding import PartitionSpec as P

STEPS = 3


HIGH = lax.Precision.HIGHEST


def gram_of(vectors):
    return jnp.einsum("bn,cn->bc", vectors, vectors, precision=HIGH)


def solve_lower(factor, vectors):
    return lax.linalg.triangular_solve(factor, vectors, left_side=True, lower=True)


def per_device(tiles, tile_slots, tile_counts, user_degree, item_degree, start_panel):
    tile_stack = tiles[0, 0].astype(jnp.float32)
    slot_list = tile_slots[0, 0]
    tile_total = tile_counts[0, 0]
    slot_count = tile_stack.shape[0]
    tile_width = tile_stack.shape[1]
    row_blocks = user_degree.shape[0] // tile_width
    col_blocks = item_degree.shape[0] // tile_width
    block_width = start_panel.shape[0]
    live_mask = jnp.arange(slot_count) < tile_total
    local_rows = slot_list // col_blocks
    local_cols = slot_list % col_blocks
    row_select = (
        (local_rows[:, None] == jnp.arange(row_blocks)[None, :]) & live_mask[:, None]
    ).astype(jnp.float32)
    col_select = (
        (local_cols[:, None] == jnp.arange(col_blocks)[None, :]) & live_mask[:, None]
    ).astype(jnp.float32)
    user_scale = lax.rsqrt(user_degree.astype(jnp.float32))
    item_scale = lax.rsqrt(item_degree.astype(jnp.float32))
    user_group = row_blocks * tile_width // lax.axis_size("col")
    item_group = col_blocks * tile_width // lax.axis_size("row")
    user_offset = lax.axis_index("col") * user_group
    item_offset = lax.axis_index("row") * item_group
    user_scale_own = lax.dynamic_slice_in_dim(user_scale, user_offset, user_group)
    item_scale_own = lax.dynamic_slice_in_dim(item_scale, item_offset, item_group)
    start_total = lax.psum(gram_of(start_panel), ("row", "col"))
    start_factor = jnp.linalg.cholesky(start_total)
    item_basis = solve_lower(start_factor, start_panel)
    user_basis = start_panel[:, :0]
    item_factor = start_factor
    user_list = []
    item_list = []
    for iteration in range(STEPS):
        scaled = item_basis * item_scale_own[None, :]
        item_full = lax.all_gather(scaled, "row", axis=1, tiled=True)
        forward_panel_blocks = item_full.reshape(block_width, col_blocks, tile_width)
        forward_chosen = jnp.take(forward_panel_blocks, local_cols, axis=1)
        forward_partial_value = jnp.einsum(
            "mrc,bmc->bmr", tile_stack, forward_chosen, precision=HIGH
        )
        forward_summed = jnp.einsum(
            "bmr,mk->bkr", forward_partial_value, row_select, precision=HIGH
        )
        forward = (
            lax.psum_scatter(
                forward_summed.reshape(block_width, row_blocks * tile_width),
                "col",
                scatter_dimension=1,
                tiled=True,
            )
            * user_scale_own[None, :]
        )
        if iteration > 0:
            forward = forward - jnp.dot(item_factor.T, user_basis, precision=HIGH)
        user_factor = jnp.linalg.cholesky(lax.psum(gram_of(forward), ("row", "col")))
        user_basis = solve_lower(user_factor, forward)
        scaled = user_basis * user_scale_own[None, :]
        user_full = lax.all_gather(scaled, "col", axis=1, tiled=True)
        panel_blocks = user_full.reshape(block_width, row_blocks, tile_width)
        chosen = jnp.take(panel_blocks, local_rows, axis=1)
        partial_value = jnp.einsum("mrc,bmr->bmc", tile_stack, chosen, precision=HIGH)
        summed = jnp.einsum("bmc,mk->bkc", partial_value, col_select, precision=HIGH)
        backward = (
            lax.psum_scatter(
                summed.reshape(block_width, col_blocks * tile_width),
                "row",
                scatter_dimension=1,
                tiled=True,
            )
            * item_scale_own[None, :]
        )
        backward = backward - jnp.dot(user_factor.T, item_basis, precision=HIGH)
        item_factor = jnp.linalg.cholesky(lax.psum(gram_of(backward), ("row", "col")))
        item_basis = solve_lower(item_factor, backward)
        user_list.append(user_factor)
        item_list.append(item_factor)
    user_total = row_blocks * tile_width * lax.axis_size("row")
    item_total = col_blocks * tile_width * lax.axis_size("col")
    return (
        math.sqrt(user_total) * user_basis,
        math.sqrt(item_total) * item_basis,
        jnp.stack(user_list),
        jnp.stack(item_list),
    )


def solution(mesh):
    in_specs = (
        P("row", "col", None, None, None),
        P("row", "col", None),
        P("row", "col"),
        P("row"),
        P("col"),
        P(None, ("col", "row")),
    )
    out_specs = (P(None, ("row", "col")), P(None, ("col", "row")), P(), P())
    return jax.shard_map(
        per_device, mesh=mesh, in_specs=in_specs, out_specs=out_specs, check_vma=False
    )
```

profile of v0, /device:TPU:0, one launch (start us, length us, event | category | flops | bytes accessed | tf_op | source)
XLA Modules:
  0.0 663.9 jit_solution(9862747009121830128)
XLA Ops:
  9.9 42.2 %psum.49 = f32[64,64]{0,1:T(8,128)S(1)} all-reduce(f32[64,64]{0,1:T(8,128)S(1)} %fusion.171), channel_id=1, replica_groups=mesh['row'=4,'col'=8] {'row','col'}, use_global_device_ids=true, to_apply=%region_0.1 | all-reduce | flops 4096 | bytes 32768 | tf_op jit(solution)/shard_map/psum | solution.py:48
  65.3 11.5 %all_gather.18 = f32[64,1536]{1,0:T(8,128)S(1)} all-gather(f32[64,384]{1,0:T(8,128)S(1)} %get-tuple-element.29), channel_id=1, replica_groups=mesh['row'=4,'col'=8] {'row'}, dimensions={1}, use_global_device_ids=true | all-gather | bytes 491520 | tf_op jit(solution)/shard_map/all_gather | solution.py:57
  82.6 29.2 %reduce-scatter.7.cloned.1.call-done = f32[64,256]{1,0:T(8,128)} async-done(((f32[64,2048]{1,0:T(8,128)}), f32[64,256]{1,0:T(8,128)}) %reduce-scatter.7.cloned.1.call-update) | async-done | bytes 65552 | tf_op jit(solution)/shard_map/reduce_scatter | solution.py:67
  112.9 38.0 %psum.50 = f32[64,64]{0,1:T(8,128)S(1)} all-reduce(f32[64,64]{0,1:T(8,128)S(1)} %fusion.56), channel_id=1, replica_groups=mesh['row'=4,'col'=8] {'row','col'}, use_global_device_ids=true, to_apply=%region_4.8 | all-reduce | flops 4096 | bytes 32768 | tf_op jit(solution)/shard_map/psum | solution.py:77
  151.1 5.8 cholesky.130
  163.4 15.9 %all_gather.19 = f32[64,2048]{1,0:T(8,128)S(1)} all-gather(f32[64,256]{1,0:T(8,128)S(1)} %get-tuple-element.31), channel_id=1, replica_groups=mesh['row'=4,'col'=8] {'col'}, dimensions={1}, use_global_device_ids=true | all-gather | bytes 589824 | tf_op jit(solution)/shard_map/all_gather | solution.py:80
  183.0 24.2 %reduce-scatter.9.cloned.1.call-done = f32[64,384]{1,0:T(8,128)} async-done(((f32[64,1536]{1,0:T(8,128)}), f32[64,384]{1,0:T(8,128)}) %reduce-scatter.9.cloned.1.call-update) | async-done | bytes 98320 | tf_op jit(solution)/shard_map/reduce_scatter | solution.py:86
  209.3 39.5 %psum.51 = f32[64,64]{0,1:T(8,128)S(1)} all-reduce(f32[64,64]{0,1:T(8,128)S(1)} %fusion.172), channel_id=1, replica_groups=mesh['row'=4,'col'=8] {'row','col'}, use_global_device_ids=true, to_apply=%region_6.12 | all-reduce | flops 4096 | bytes 32768 | tf_op jit(solution)/shard_map/psum | solution.py:95
  248.9 5.8 cholesky.141
  261.3 11.5 %all_gather.20 = f32[64,1536]{1,0:T(8,128)S(1)} all-gather(f32[64,384]{1,0:T(8,128)S(1)} %get-tuple-element.33), channel_id=1, replica_groups=mesh['row'=4,'col'=8] {'row'}, dimensions={1}, use_global_device_ids=true | all-gather | bytes 491520 | tf_op jit(solution)/shard_map/all_gather | solution.py:57
  277.7 30.1 %reduce-scatter.11.cloned.1.call-done = f32[64,256]{1,0:T(8,128)} async-done(((f32[64,2048]{1,0:T(8,128)}), f32[64,256]{1,0:T(8,128)}) %reduce-scatter.11.cloned.1.call-update) | async-done | bytes 65552 | tf_op jit(solution)/shard_map/reduce_scatter | solution.py:67
  309.7 38.2 %psum.52 = f32[64,64]{0,1:T(8,128)S(1)} all-reduce(f32[64,64]{0,1:T(8,128)S(1)} %fusion.173), channel_id=1, replica_groups=mesh['row'=4,'col'=8] {'row','col'}, use_global_device_ids=true, to_apply=%region_8.14 | all-reduce | flops 4096 | bytes 32768 | tf_op jit(solution)/shard_map/psum | solution.py:77
  348.1 5.8 cholesky.152
  360.4 15.7 %all_gather.21 = f32[64,2048]{1,0:T(8,128)S(1)} all-gather(f32[64,256]{1,0:T(8,128)S(1)} %get-tuple-element.35), channel_id=1, replica_groups=mesh['row'=4,'col'=8] {'col'}, dimensions={1}, use_global_device_ids=true | all-gather | bytes 589824 | tf_op jit(solution)/shard_map/all_gather | solution.py:80
  379.8 24.2 %reduce-scatter.13.cloned.1.call-done = f32[64,384]{1,0:T(8,128)} async-done(((f32[64,1536]{1,0:T(8,128)}), f32[64,384]{1,0:T(8,128)}) %reduce-scatter.13.cloned.1.call-update) | async-done | bytes 98320 | tf_op jit(solution)/shard_map/reduce_scatter | solution.py:86
  406.1 39.5 %psum.53 = f32[64,64]{0,1:T(8,128)S(1)} all-reduce(f32[64,64]{0,1:T(8,128)S(1)} %fusion.174), channel_id=1, replica_groups=mesh['row'=4,'col'=8] {'row','col'}, use_global_device_ids=true, to_apply=%region_10.16 | all-reduce | flops 4096 | bytes 32768 | tf_op jit(solution)/shard_map/psum | solution.py:95
  445.7 5.8 cholesky.163
  458.1 11.5 %all_gather.22 = f32[64,1536]{1,0:T(8,128)S(1)} all-gather(f32[64,384]{1,0:T(8,128)S(1)} %get-tuple-element.37), channel_id=1, replica_groups=mesh['row'=4,'col'=8] {'row'}, dimensions={1}, use_global_device_ids=true | all-gather | bytes 491520 | tf_op jit(solution)/shard_map/all_gather | solution.py:57
  474.8 29.8 %reduce-scatter.15.cloned.1.call-done = f32[64,256]{1,0:T(8,128)} async-done(((f32[64,2048]{1,0:T(8,128)}), f32[64,256]{1,0:T(8,128)}) %reduce-scatter.15.cloned.1.call-update) | async-done | bytes 65552 | tf_op jit(solution)/shard_map/reduce_scatter | solution.py:67
  506.5 38.0 %psum.54 = f32[64,64]{0,1:T(8,128)S(1)} all-reduce(f32[64,64]{0,1:T(8,128)S(1)} %fusion.175), channel_id=1, replica_groups=mesh['row'=4,'col'=8] {'row','col'}, use_global_device_ids=true, to_apply=%region_12.18 | all-reduce | flops 4096 | bytes 32768 | tf_op jit(solution)/shard_map/psum | solution.py:77
  544.7 5.8 cholesky.174
  557.6 15.7 %all_gather.23 = f32[64,2048]{1,0:T(8,128)S(1)} all-gather(f32[64,256]{1,0:T(8,128)S(1)} %get-tuple-element.13), channel_id=1, replica_groups=mesh['row'=4,'col'=8] {'col'}, dimensions={1}, use_global_device_ids=true | all-gather | bytes 589824 | tf_op jit(solution)/shard_map/all_gather | solution.py:80
  577.7 23.6 %reduce-scatter.17.cloned.1.call-done = f32[64,384]{1,0:T(8,128)} async-done(((f32[64,1536]{1,0:T(8,128)}), f32[64,384]{1,0:T(8,128)}) %reduce-scatter.17.cloned.1.call-update) | async-done | bytes 98320 | tf_op jit(solution)/shard_map/reduce_scatter | solution.py:86
  603.3 39.5 %psum.55 = f32[64,64]{0,1:T(8,128)S(1)} all-reduce(f32[64,64]{0,1:T(8,128)S(1)} %fusion.176), channel_id=1, replica_groups=mesh['row'=4,'col'=8] {'row','col'}, use_global_device_ids=true, to_apply=%region_14.20 | all-reduce | flops 4096 | bytes 32768 | tf_op jit(solution)/shard_map/psum | solution.py:95
  (122 shorter events, 101.1 us)
Async XLA Ops:
  7.2 70.3 %copy-start = (bf16[1,1,32,128,128]{4,3,2,1,0:T(8,128)(2,1)S(1)}, bf16[1,1,32,128,128]{4,3,2,1,0:T(8,128)(2,1)}, u32[]{:S(2)}) copy-start(bf16[1,1,32,128,128]{4,3,2,1,0:T(8,128)(2,1)} %param.15) | copy-start | bytes 3145732
  7.2 104.6 %reduce-scatter.7.cloned.1.call-start = ((), (), s32[]{:S(2)}) async-start(), calls=%async_computation.6 | async-start | bytes 589824 | tf_op jit(solution)/shard_map/reduce_scatter | solution.py:67
  8.0 0.7 copy-start.3
  52.1 12.9 %copy-start.1 = (f32[64,384]{1,0:T(8,128)S(1)}, f32[64,384]{1,0:T(8,128)}, u32[]{:S(2)}) copy-start(f32[64,384]{1,0:T(8,128)} %param.20) | copy-start | bytes 294916
  81.7 125.5 %reduce-scatter.9.cloned.1.call-start = ((), (), s32[]{:S(2)}) async-start(), calls=%async_computation.7 | async-start | bytes 491520 | tf_op jit(solution)/shard_map/reduce_scatter | solution.py:86
  156.9 6.2 copy-start.2
  183.0 124.8 %reduce-scatter.11.cloned.1.call-start = ((), (), s32[]{:S(2)}) async-start(), calls=%async_computation.8 | async-start | bytes 589824 | tf_op jit(solution)/shard_map/reduce_scatter | solution.py:67
  277.7 126.3 %reduce-scatter.13.cloned.1.call-start = ((), (), s32[]{:S(2)}) async-start(), calls=%async_computation.9 | async-start | bytes 491520 | tf_op jit(solution)/shard_map/reduce_scatter | solution.py:86
  379.8 124.8 %reduce-scatter.15.cloned.1.call-start = ((), (), s32[]{:S(2)}) async-start(), calls=%async_computation.10 | async-start | bytes 589824 | tf_op jit(solution)/shard_map/reduce_scatter | solution.py:67
  474.5 126.7 %reduce-scatter.17.cloned.1.call-start = ((), (), s32[]{:S(2)}) async-start(), calls=%async_computation.11 | async-start | bytes 491520 | tf_op jit(solution)/shard_map/reduce_scatter | solution.py:86
Sparse Core Ops, SparseCore 0:
  81.8 29.9 reduce-scatter.6
  183.1 24.0 reduce-scatter.8
  277.8 29.9 reduce-scatter.10
  379.9 24.0 reduce-scatter.12
  474.6 29.9 reduce-scatter.14
  577.1 24.0 reduce-scatter.16
where the time goes:
time: 672 us; the launch traced here: 664 us
  blocking collectives  357 us (53%)
  waiting for transfers between devices  161 us (24%)
  other arithmetic  87.4 us (13%)
  matrix products  31.8 us (5%)
  between operations  15.9 us (2%)
  local copies, waits for them, and re-layouts  10.5 us (2%)
    psum x3, blocking collectives, per_device(): lax.psum(gram_of(backward), ('row', 'col'))  119 us
    psum x3, blocking collectives, per_device(): lax.psum(gram_of(forward), ('row', 'col'))  114 us
    reduce_scatter x3, waiting for transfers between devices, per_device(): lax.psum_scatter(forward_summed.reshape(block_width, row_blocks * tile_wi...  89.1 us
    reduce_scatter x3, waiting for transfers between devices, per_device(): lax.psum_scatter(summed.reshape(block_width, col_blocks * tile_width), 'r...  71.9 us
    all_gather x3, blocking collectives, per_device(): user_full = lax.all_gather(scaled, 'col', axis=1, tiled=True)  47.3 us
    psum x1, blocking collectives, per_device(): start_total = lax.psum(gram_of(start_panel), ('row', 'col'))  42.2 us
    another operation x8, other arithmetic, solve_lower(): lax.linalg.triangular_solve(factor, vectors, left_side=True, lower=True)  34.9 us
    all_gather x3, blocking collectives, per_device(): item_full = lax.all_gather(scaled, 'row', axis=1, tiled=True)  34.4 us
  transfers between devices with their start and end apart: 6, of which 6 were waited for; matrix products, arithmetic and copies ran while one was open for 0% of the time, Pallas kernels for 0%

commit v1 on v0

--- a/solution.py
+++ b/solution.py
@@ -1,8 +1,11 @@
+import functools
 import math
 
 import jax
 import jax.numpy as jnp
 from jax import lax
+from jax.experimental import pallas as pl
+from jax.experimental.pallas import tpu as pltpu
 from jax.sharding import PartitionSpec as P
 
 STEPS = 3
@@ -19,7 +22,7 @@
     return lax.linalg.triangular_solve(factor, vectors, left_side=True, lower=True)
 
 
-def per_device(tiles, tile_slots, tile_counts, user_degree, item_degree, start_panel):
+def per_device_arrays(tiles, tile_slots, tile_counts, user_degree, item_degree, start_panel):
     tile_stack = tiles[0, 0].astype(jnp.float32)
     slot_list = tile_slots[0, 0]
     tile_total = tile_counts[0, 0]
@@ -106,6 +109,480 @@
     )
 
 
+MESH = pl.DeviceIdType.MESH
+NT = (((1,), (1,)), ((), ()))
+NN = (((1,), (0,)), ((), ()))
+
+
+def dot_high(a, b, dims=NN):
+    return lax.dot_general(
+        a, b, dims, precision=HIGH, preferred_element_type=jnp.float32
+    )
+
+
+def factor_and_inverse(gram):
+    n = gram.shape[0]
+    blocks = n // 8
+    eye = (
+        lax.broadcasted_iota(jnp.int32, (n, n), 0)
+        == lax.broadcasted_iota(jnp.int32, (n, n), 1)
+    ).astype(jnp.float32)
+    work = jnp.concatenate([gram, eye], axis=1)
+    sub = lax.broadcasted_iota(jnp.int32, (8, 2 * n), 0)
+
+    def block_step(b, parts):
+        parts = list(parts)
+        live = [None] + [
+            (jnp.zeros((8, 2 * n), jnp.int32) + b < blocks - i).astype(jnp.float32)
+            for i in range(1, blocks)
+        ]
+        for s in range(8):
+            column = jnp.broadcast_to(parts[0][:, s : s + 1], (8, 2 * n))
+            pivot = jnp.broadcast_to(column[s : s + 1, :], (8, 2 * n))
+            scale = lax.rsqrt(pivot)
+            row = jnp.broadcast_to(parts[0][s : s + 1, :], (8, 2 * n)) * scale
+            for i in range(1, blocks):
+                other = jnp.broadcast_to(parts[i][:, s : s + 1], (8, 2 * n))
+                parts[i] = parts[i] - (other * live[i]) * (row * scale)
+            below = parts[0] - (column * scale) * row
+            parts[0] = jnp.where(sub > s, below, jnp.where(sub == s, row, parts[0]))
+        parts = [pltpu.roll(p, 2 * n - 8, 1) for p in parts]
+        return tuple(parts[1:] + parts[:1])
+
+    parts = tuple(work[8 * i : 8 * i + 8] for i in range(blocks))
+    parts = lax.fori_loop(0, blocks, block_step, parts)
+    work = jnp.concatenate(parts, axis=0)
+    upper = lax.broadcasted_iota(jnp.int32, (n, n), 0) <= lax.broadcasted_iota(
+        jnp.int32, (n, n), 1
+    )
+    return jnp.where(upper, work[:, n:], 0.0), work[:, :n]
+
+
+def kernel(
+    n_row,
+    n_col,
+    row_blocks,
+    col_blocks,
+    index_ref,
+    tiles_ref,
+    user_degree_ref,
+    item_degree_ref,
+    start_ref,
+    left_ref,
+    right_ref,
+    left_factor_ref,
+    right_factor_ref,
+    item_all,
+    user_all,
+    split,
+    running,
+    user_send,
+    sibling_in,
+    user_send2,
+    user_in,
+    item_send,
+    item_in,
+    item_raw,
+    item_basis,
+    user_basis,
+    gram_own,
+    gram_row,
+    gram_sum,
+    gram_col,
+    s_gr,
+    r_gr,
+    s_gc,
+    r_gc,
+    s_ir,
+    r_ir,
+    s_uz,
+    r_uz,
+    s_us,
+    r_us,
+    s_sib,
+    r_sib,
+    s_z,
+    r_z,
+    s_row,
+    r_row,
+):
+    row = lax.axis_index("row")
+    col = lax.axis_index("col")
+    n_z = n_col // 2
+    core = lax.rem(col, 2)
+    z = col // 2
+    sibling = col + 1 - 2 * core
+    slots = tiles_ref.shape[0]
+    width = tiles_ref.shape[1]
+    block = start_ref.shape[0]
+    half = block // 2
+    user_group = user_all.shape[2]
+    item_group = item_all.shape[2]
+    user_per = user_group // width
+    item_per = item_group // width
+
+    barrier = pltpu.get_barrier_semaphore()
+    for d in range(1, n_row):
+        pl.semaphore_signal(
+            barrier, inc=1, device_id=(lax.rem(row + d, n_row), col), device_id_type=MESH
+        )
+    for d in range(1, n_col):
+        pl.semaphore_signal(
+            barrier, inc=1, device_id=(row, lax.rem(col + d, n_col)), device_id_type=MESH
+        )
+    pl.semaphore_wait(barrier, n_row + n_col - 2)
+
+    def send(src, dst, s_sem, r_sem, target):
+        copy = pltpu.make_async_remote_copy(
+            src_ref=src,
+            dst_ref=dst,
+            send_sem=s_sem,
+            recv_sem=r_sem,
+            device_id=target,
+            device_id_type=MESH,
+        )
+        copy.start()
+        return copy
+
+    user_scale = lax.rsqrt(user_degree_ref[pl.ds(col, 1), :].astype(jnp.float32))
+    item_scale = lax.rsqrt(item_degree_ref[pl.ds(row, 1), :].astype(jnp.float32))
+
+    def gram_start(raw, way):
+        gram = dot_high(raw, raw, NT)
+        gram_own[way] = jnp.concatenate([gram[:half], gram[half:]], axis=1)
+        copies = []
+        for d in range(1, n_row):
+            copies.append(
+                send(
+                    gram_own.at[way],
+                    gram_row.at[way, d],
+                    s_gr.at[way, d],
+                    r_gr.at[way, d],
+                    (lax.rem(row + d, n_row), col),
+                )
+            )
+        return copies
+
+    def gram_middle(copies, way):
+        gram_row[way, 0] = gram_own[way]
+        for copy in copies:
+            copy.wait_recv()
+        total = gram_row[way, row]
+        for i in range(1, n_row):
+            total = total + gram_row[way, lax.rem(row - i + n_row, n_row)]
+        gram_sum[way] = total
+        out = []
+        for d in range(1, n_col):
+            out.append(
+                send(
+                    gram_sum.at[way],
+                    gram_col.at[way, d],
+                    s_gc.at[way, d],
+                    r_gc.at[way, d],
+                    (row, lax.rem(col + d, n_col)),
+                )
+            )
+        return out
+
+    def gram_end(copies, way):
+        for copy in copies:
+            copy.wait_recv()
+        total = jnp.zeros((half, 2 * block), jnp.float32)
+        gram_col[way, 0] = gram_sum[way]
+        for j in range(n_col):
+            total = total + gram_col[way, lax.rem(col - j + n_col, n_col)]
+        gram = jnp.concatenate([total[:, :block], total[:, block:]], axis=0)
+        return factor_and_inverse(gram)
+
+    def put_split(first_block, values):
+        for b in range(values.shape[1] // width):
+            part = values[:, b * width : (b + 1) * width]
+            high = part.astype(jnp.bfloat16)
+            low = (part - high.astype(jnp.float32)).astype(jnp.bfloat16)
+            split[first_block + b] = jnp.concatenate([high, low], axis=0)
+
+    def products(base, dims):
+        def one(t, total):
+            tile = tiles_ref[index_ref[base + t]]
+            vectors = split[index_ref[base + slots + t]]
+            keep = index_ref[base + 2 * slots + t].astype(jnp.float32)
+            both = lax.dot_general(
+                vectors, tile, dims, preferred_element_type=jnp.float32
+            )
+            total = total * keep + (both[:block] + both[block:])
+            running[t] = total
+            return total
+
+        lax.fori_loop(
+            0, slots, one, jnp.zeros((block, width), jnp.float32), unroll=4
+        )
+
+    running[slots] = jnp.zeros((block, width), jnp.float32)
+    forward_base = 0
+    forward_last = 3 * slots
+    backward_base = forward_last + row_blocks
+    backward_last = backward_base + 3 * slots
+
+    item_raw[...] = start_ref[...]
+    user_basis[...] = jnp.zeros_like(user_basis)
+
+    def step(k, carry):
+        raw = item_raw[...]
+        sent = gram_start(raw, 0)
+        scaled = raw * item_scale
+        item_all[row] = scaled
+        moved = []
+        for d in range(1, n_row):
+            moved.append(
+                send(
+                    item_all.at[row],
+                    item_all.at[row],
+                    s_ir.at[d],
+                    r_ir.at[d],
+                    (lax.rem(row + d, n_row), col),
+                )
+            )
+        put_split(row * item_per, scaled)
+        sent2 = gram_middle(sent, 0)
+        for d in range(1, n_row):
+            moved[d - 1].wait_recv()
+            source = lax.rem(row - d + n_row, n_row)
+            put_split(source * item_per, item_all[source])
+        products(forward_base, NT)
+        pair = []
+        for core_at in range(2):
+            for z_at in range(n_z):
+                for b in range(user_per):
+                    user_send[core_at * n_z + z_at, :, b * width : (b + 1) * width] = (
+                        running[
+                            index_ref[
+                                forward_last + (z_at * 2 + core_at) * user_per + b
+                            ]
+                        ]
+                    )
+        for d in list(range(1, n_z)) + [0]:
+            target_z = lax.rem(z + d, n_z)
+            pair.append(
+                send(
+                    user_send.at[(1 - core) * n_z + target_z],
+                    sibling_in.at[target_z],
+                    s_sib.at[d],
+                    r_sib.at[d],
+                    (row, sibling),
+                )
+            )
+        across = []
+        for d in range(1, n_z):
+            target_z = lax.rem(z + d, n_z)
+            pair[d - 1].wait_recv()
+            user_send2[target_z] = (
+                user_send[core * n_z + target_z] + sibling_in[target_z]
+            )
+            across.append(
+                send(
+                    user_send2.at[target_z],
+                    user_in.at[z],
+                    s_z.at[d],
+                    r_z.at[d],
+                    (row, target_z * 2 + core),
+                )
+            )
+        pair[n_z - 1].wait_recv()
+        summed = user_send[core * n_z + z] + sibling_in[z]
+        factor_t, inverse = gram_end(sent2, 0)
+        right_factor_ref[lax.rem(k + STEPS - 1, STEPS)] = factor_t.T
+        item_basis[...] = dot_high(inverse, raw)
+        correction = dot_high(factor_t, user_basis[...])
+        for d in range(1, n_z):
+            across[d - 1].wait_recv()
+            summed = summed + user_in[lax.rem(z - d + n_z, n_z)]
+        forward = dot_high(inverse, summed * user_scale) - correction
+        for copy in sent + sent2 + moved + pair + across:
+            copy.wait_send()
+
+        sent = gram_start(forward, 1)
+        scaled = forward * user_scale
+        user_all[col] = scaled
+        moved = []
+        for d in range(1, n_z):
+            moved.append(
+                send(
+                    user_all.at[col],
+                    user_all.at[col],
+                    s_uz.at[d],
+                    r_uz.at[d],
+                    (row, lax.rem(z + d, n_z) * 2 + core),
+                )
+            )
+        passed = [
+            send(
+                user_all.at[col],
+                user_all.at[col],
+                s_us.at[0],
+                r_us.at[0],
+                (row, sibling),
+            )
+        ]
+        put_split(col * user_per, scaled)
+        sent2 = gram_middle(sent, 1)
+        passed[0].wait_recv()
+        put_split(sibling * user_per, user_all[sibling])
+        for d in range(1, n_z):
+            moved[d - 1].wait_recv()
+            source = lax.rem(z - d + n_z, n_z) * 2 + core
+            passed.append(
+                send(
+                    user_all.at[source],
+                    user_all.at[source],
+                    s_us.at[d],
+                    r_us.at[d],
+                    (row, sibling),
+                )
+            )
+            put_split(source * user_per, user_all[source])
+        for d in range(1, n_z):
+            passed[d].wait_recv()
+            source = lax.rem(z - d + n_z, n_z) * 2 + 1 - core
+            put_split(source * user_per, user_all[source])
+        products(backward_base, NN)
+        for j in range(n_row):
+            for b in range(item_per):
+                item_send[j, :, b * width : (b + 1) * width] = running[
+                    index_ref[backward_last + j * item_per + b]
+                ]
+        across = []
+        for d in range(1, n_row):
+            target = lax.rem(row + d, n_row)
+            across.append(
+                send(
+                    item_send.at[target],
+                    item_in.at[row],
+                    s_row.at[d],
+                    r_row.at[d],
+                    (target, col),
+                )
+            )
+        factor_t, inverse = gram_end(sent2, 1)
+        left_factor_ref[k] = factor_t.T
+        user_basis[...] = dot_high(inverse, forward)
+        correction = dot_high(factor_t, item_basis[...])
+        summed = item_send[row]
+        for d in range(1, n_row):
+            across[d - 1].wait_recv()
+            summed = summed + item_in[lax.rem(row - d + n_row, n_row)]
+        item_raw[...] = dot_high(inverse, summed * item_scale) - correction
+        for copy in sent + sent2 + moved + passed + across:
+            copy.wait_send()
+        return carry
+
+    lax.fori_loop(0, STEPS, step, 0)
+
+    raw = item_raw[...]
+    sent = gram_start(raw, 0)
+    left_ref[...] = user_basis[...] * math.sqrt(row_blocks * width * n_row)
+    sent2 = gram_middle(sent, 0)
+    factor_t, inverse = gram_end(sent2, 0)
+    right_factor_ref[STEPS - 1] = factor_t.T
+    right_ref[...] = dot_high(inverse, raw) * math.sqrt(col_blocks * width * n_col)
+    for copy in sent + sent2:
+        copy.wait_send()
+
+
+def order_tables(keys, partners, live, blocks):
+    slots = keys.shape[0]
+    at = jnp.arange(slots)
+    rank_key = jnp.where(live, keys, blocks) * slots + at
+    rank = jnp.sum((rank_key[None, :] < rank_key[:, None]).astype(jnp.int32), axis=1)
+    placed = rank[None, :] == at[:, None]
+    order = jnp.sum(jnp.where(placed, at[None, :], 0), axis=1)
+    partner = jnp.sum(jnp.where(placed, partners[None, :], 0), axis=1)
+    same = (keys[None, :] == keys[:, None]) & (live[None, :] & live[:, None])
+    earlier = jnp.any(same & (at[None, :] < at[:, None]), axis=1)
+    keep = jnp.sum(jnp.where(placed, earlier[None, :].astype(jnp.int32), 0), axis=1)
+    mine = (keys[None, :] == jnp.arange(blocks)[:, None]) & live[None, :]
+    last = jnp.max(jnp.where(mine, rank[None, :], -1), axis=1)
+    last = jnp.where(last < 0, slots, last)
+    return [order, partner, keep, last]
+
+
+def per_device(tiles, tile_slots, tile_counts, user_degree, item_degree, start_panel):
+    n_row, n_col = lax.axis_size("row"), lax.axis_size("col")
+    slots, width = tiles.shape[2], tiles.shape[3]
+    block = start_panel.shape[0]
+    row_blocks = user_degree.shape[0] // width
+    col_blocks = item_degree.shape[0] // width
+    user_group = user_degree.shape[0] // n_col
+    item_group = item_degree.shape[0] // n_row
+    slot_list = tile_slots[0, 0]
+    live = jnp.arange(slots) < tile_counts[0, 0]
+    slot_list = jnp.where(live, slot_list, 0)
+    local_rows, local_cols = slot_list // col_blocks, slot_list % col_blocks
+    index = jnp.concatenate(
+        order_tables(local_rows, local_cols, live, row_blocks)
+        + order_tables(local_cols, local_rows, live, col_blocks)
+    ).astype(jnp.int32)
+    vmem = pl.BlockSpec(memory_space=pltpu.VMEM)
+    f32 = jnp.float32
+    dma = pltpu.SemaphoreType.DMA
+    n_z = n_col // 2
+    out = pl.pallas_call(
+        functools.partial(kernel, n_row, n_col, row_blocks, col_blocks),
+        out_shape=(
+            jax.ShapeDtypeStruct((block, user_group), f32),
+            jax.ShapeDtypeStruct((block, item_group), f32),
+            jax.ShapeDtypeStruct((STEPS, block, block), f32),
+            jax.ShapeDtypeStruct((STEPS, block, block), f32),
+        ),
+        in_specs=[pl.BlockSpec(memory_space=pltpu.SMEM)] + [vmem] * 4,
+        out_specs=(vmem,) * 4,
+        scratch_shapes=[
+            pltpu.VMEM((n_row, block, item_group), f32),
+            pltpu.VMEM((n_col, block, user_group), f32),
+            pltpu.VMEM((max(row_blocks, col_blocks), 2 * block, width), jnp.bfloat16),
+            pltpu.VMEM((slots + 1, block, width), f32),
+            pltpu.VMEM((n_col, block, user_group), f32),
+            pltpu.VMEM((n_z, block, user_group), f32),
+            pltpu.VMEM((n_z, block, user_group), f32),
+            pltpu.VMEM((n_z, block, user_group), f32),
+            pltpu.VMEM((n_row, block, item_group), f32),
+            pltpu.VMEM((n_row, block, item_group), f32),
+            pltpu.VMEM((block, item_group), f32),
+            pltpu.VMEM((block, item_group), f32),
+            pltpu.VMEM((block, user_group), f32),
+            pltpu.VMEM((2, block // 2, 2 * block), f32),
+            pltpu.VMEM((2, n_row, block // 2, 2 * block), f32),
+            pltpu.VMEM((2, block // 2, 2 * block), f32),
+            pltpu.VMEM((2, n_col, block // 2, 2 * block), f32),
+            dma((2, n_row)),
+            dma((2, n_row)),
+            dma((2, n_col)),
+            dma((2, n_col)),
+            dma((n_row,)),
+            dma((n_row,)),
+            dma((n_z,)),
+            dma((n_z,)),
+            dma((n_z,)),
+            dma((n_z,)),
+            dma((n_z,)),
+            dma((n_z,)),
+            dma((n_z,)),
+            dma((n_z,)),
+            dma((n_row,)),
+            dma((n_row,)),
+        ],
+        compiler_params=pltpu.CompilerParams(
+            collective_id=0, has_side_effects=True, vmem_limit_bytes=32 * 1024 * 1024
+        ),
+    )(
+        index,
+        tiles[0, 0],
+        user_degree.reshape(n_col, user_group),
+        item_degree.reshape(n_row, item_group),
+        start_panel,
+    )
+    return tuple(out)
+
+
 def solution(mesh):
     in_specs = (
         P("row", "col", None, None, None),
@@ -116,6 +593,15 @@
         P(None, ("col", "row")),
     )
     out_specs = (P(None, ("row", "col")), P(None, ("col", "row")), P(), P())
-    return jax.shard_map(
-        per_device, mesh=mesh, in_specs=in_specs, out_specs=out_specs, check_vma=False
-    )
+    def whole(*args):
+        tile_width = args[0].shape[3]
+        cells = mesh.shape["row"] * mesh.shape["col"]
+        owned = (args[3].shape[0] // cells, args[4].shape[0] // cells)
+        form = per_device
+        if owned[0] % tile_width or owned[1] % tile_width:
+            form = per_device_arrays
+        return jax.shard_map(
+            form, mesh=mesh, in_specs=in_specs, out_specs=out_specs, check_vma=False
+        )(*args)
+
+    return whole

time: 672 us -> 148 us (0.22); the launches traced: 664 us -> 147 us
  blocking collectives: 357 us -> 0 us
  waiting for transfers between devices: 161 us -> 0 us
  Pallas kernels: 0 us -> 138 us
  other arithmetic: 87.4 us -> 1.02 us
  matrix products: 31.8 us -> 0 us
  between operations: 15.9 us -> 1.34 us
    psum x7 -> x0, blocking collectives: 275 us -> none  [the longest x3 119 us: per_device(): lax.psum(gram_of(backward), ('row', 'col'))]
    reduce_scatter x6 -> x0, waiting for transfers between devices: 161 us -> none  [the longest x3 89.1 us: per_device(): lax.psum_scatter(forward_summed.reshape(block_width, row_blocks * tile_wi...]
    pallas_call x0 -> x1, Pallas kernels: none -> 138 us  [per_device(): pl.pallas_call(functools.partial(kernel, n_row, n_col, row_blocks, col_bl...]
    another operation x37 -> x0, other arithmetic: 85.8 us -> none  [the longest x8 34.9 us: solve_lower(): lax.linalg.triangular_solve(factor, vectors, left_side=True, lower=True)]
    all_gather x6 -> x0, blocking collectives: 81.7 us -> none  [the longest x3 47.3 us: per_device(): user_full = lax.all_gather(scaled, 'col', axis=1, tiled=True)]
    dot_general x24 -> x0, matrix products: 28.5 us -> none  [the longest x3 6.51 us: per_device(): jnp.einsum('mrc,bmc->bmr', tile_stack, forward_chosen, precision=HIGH)]
  transfers between devices with their start and end apart: 6 -> 0, of which waited for: 6 -> 0; matrix products, arithmetic and copies ran while one was open for 0% -> 0% of each run, Pallas kernels for 0% -> 0%
where the time goes in v1:
time: 148 us; the launch traced here: 147 us
  Pallas kernels  138 us (93%)
  local copies, waits for them, and re-layouts  6.7 us (5%)
    pallas_call x1, Pallas kernels, per_device(): pl.pallas_call(functools.partial(kernel, n_row, n_col, row_blocks, col_bl...  138 us
    unnamed x14, local copies, waits for them, and re-layouts  6.61 us

profile of v1, /device:TPU:0, one launch (start us, length us, event | category | flops | bytes accessed | tf_op | source)
XLA Modules:
  0.0 147.5 jit_solution(9371321516598075301)
XLA Ops:
  1.3 0.0 copy-start.4
  1.3 0.6 copy-done.4
  2.0 0.2 convert_reduce_fusion.1
  2.1 0.2 convert_reduce_fusion
  2.3 0.1 select_reduce_fusion.6
  2.5 0.1 select_reduce_fusion.7
  2.6 0.2 fusion.3
  2.8 0.2 select_reduce_fusion
  3.0 0.0 copy-start.2
  3.0 0.1 concatenate.3.index_ref
  3.1 0.6 copy-done.2
  3.7 0.0 copy-start.3
  3.7 0.7 copy-done.3
  4.4 0.0 copy-start
  4.4 1.2 copy-done
  5.6 0.0 copy-start.1
  5.6 0.9 copy-done.1
  6.5 138.4 %shard_map.93 = (f32[64,256]{1,0:T(8,128)S(1)}, f32[64,384]{1,0:T(8,128)S(1)}, f32[3,64,64]{2,1,0:T(8,128)S(1)}, f32[3,64,64]{2,1,0:T(8,128)S(1)}) custom-call(s32[220]{0:T(256)S(1)} %concatenate.3.index_ref, bf16[32,128,128]{2,1,0:T(8,128)(2,1)S(1)} %bitcast.12, s32[8,256]{1,0:T(8,128)S(1)} %reshape.124.user_degree_ref, ...), custom_call_target="tpu_custom_call" | custom-call | tf_op jit(solution)/shard_map/pallas_call | solution.py:528
  144.9 0.6 copy.15
  145.6 0.6 copy.16
  146.2 0.6 copy.17
  146.8 0.6 copy.18
  (8 shorter events, 0.1 us)
Async XLA Ops:
  1.3 0.7 copy-start.4
  3.0 0.7 copy-start.2
  3.7 0.7 copy-start.3
  4.4 1.2 copy-start
  5.6 0.9 copy-start.1

commit v2 on v1

--- a/solution.py
+++ b/solution.py
@@ -136,16 +136,27 @@
             (jnp.zeros((8, 2 * n), jnp.int32) + b < blocks - i).astype(jnp.float32)
             for i in range(1, blocks)
         ]
+        head = parts[0]
+        wide = (8, 2 * n)
+        columns = [jnp.broadcast_to(head[:, s : s + 1], wide) for s in range(8)]
+        others = [
+            [jnp.broadcast_to(parts[i][:, s : s + 1], wide) * live[i] for s in range(8)]
+            for i in range(1, blocks)
+        ]
         for s in range(8):
-            column = jnp.broadcast_to(parts[0][:, s : s + 1], (8, 2 * n))
-            pivot = jnp.broadcast_to(column[s : s + 1, :], (8, 2 * n))
-            scale = lax.rsqrt(pivot)
-            row = jnp.broadcast_to(parts[0][s : s + 1, :], (8, 2 * n)) * scale
+            scale = lax.rsqrt(jnp.broadcast_to(columns[s][s : s + 1, :], wide))
+            row = jnp.broadcast_to(head[s : s + 1, :], wide) * scale
+            below = jnp.where(sub > s, columns[s] * scale, 0.0)
+            head = jnp.where(sub == s, row, head - below * row)
+            factors = [other[s] * scale for other in others]
+            for t in range(s + 1, 8):
+                across = jnp.broadcast_to(columns[t][s : s + 1, :], wide) * scale
+                columns[t] = columns[t] - below * across
+                for other, factor in zip(others, factors):
+                    other[t] = other[t] - factor * across
             for i in range(1, blocks):
-                other = jnp.broadcast_to(parts[i][:, s : s + 1], (8, 2 * n))
-                parts[i] = parts[i] - (other * live[i]) * (row * scale)
-            below = parts[0] - (column * scale) * row
-            parts[0] = jnp.where(sub > s, below, jnp.where(sub == s, row, parts[0]))
+                parts[i] = parts[i] - factors[i - 1] * row
+        parts[0] = head
         parts = [pltpu.roll(p, 2 * n - 8, 1) for p in parts]
         return tuple(parts[1:] + parts[:1])
 
@@ -314,7 +325,7 @@
             return total
 
         lax.fori_loop(
-            0, slots, one, jnp.zeros((block, width), jnp.float32), unroll=4
+            0, slots, one, jnp.zeros((block, width), jnp.float32), unroll=8
         )
 
     running[slots] = jnp.zeros((block, width), jnp.float32)
@@ -328,7 +339,6 @@
 
     def step(k, carry):
         raw = item_raw[...]
-        sent = gram_start(raw, 0)
         scaled = raw * item_scale
         item_all[row] = scaled
         moved = []
@@ -342,12 +352,13 @@
                     (lax.rem(row + d, n_row), col),
                 )
             )
+        sent = gram_start(raw, 0)
         put_split(row * item_per, scaled)
-        sent2 = gram_middle(sent, 0)
         for d in range(1, n_row):
             moved[d - 1].wait_recv()
             source = lax.rem(row - d + n_row, n_row)
             put_split(source * item_per, item_all[source])
+        sent2 = gram_middle(sent, 0)
         products(forward_base, NT)
         pair = []
         for core_at in range(2):
@@ -400,7 +411,6 @@
         for copy in sent + sent2 + moved + pair + across:
             copy.wait_send()
 
-        sent = gram_start(forward, 1)
         scaled = forward * user_scale
         user_all[col] = scaled
         moved = []
@@ -423,6 +433,7 @@
                 (row, sibling),
             )
         ]
+        sent = gram_start(forward, 1)
         put_split(col * user_per, scaled)
         sent2 = gram_middle(sent, 1)
         passed[0].wait_recv()

time: 148 us -> 130 us (0.88)
  Pallas kernels: 138 us -> 121 us
    pallas_call x1, Pallas kernels: 138 us -> 121 us  [per_device(): pl.pallas_call(functools.partial(kernel, n_row, n_col, row_blocks, col_bl...]
where the time goes in v2:
time: 130 us
  Pallas kernels  121 us (93%)
  local copies, waits for them, and re-layouts  6.7 us (5%)
  between operations  1.34 us (1%)
    pallas_call x1, Pallas kernels, per_device(): pl.pallas_call(functools.partial(kernel, n_row, n_col, row_blocks, col_bl...  121 us
    unnamed x14, local copies, waits for them, and re-layouts  6.61 us

profile of v2, /device:TPU:0, one launch (start us, length us, event | category | flops | bytes accessed | tf_op | source)
XLA Modules:
  0.0 129.7 jit_solution(16843107746408558674)
XLA Ops:
  1.3 0.0 copy-start.4
  1.3 0.6 copy-done.4
  2.0 0.2 convert_reduce_fusion.1
  2.1 0.2 convert_reduce_fusion
  2.3 0.1 select_reduce_fusion.6
  2.5 0.1 select_reduce_fusion.7
  2.6 0.2 fusion.3
  2.8 0.2 select_reduce_fusion
  3.0 0.0 copy-start.2
  3.0 0.1 concatenate.3.index_ref
  3.1 0.6 copy-done.2
  3.7 0.0 copy-start.3
  3.7 0.7 copy-done.3
  4.4 0.0 copy-start
  4.4 1.2 copy-done
  5.6 0.0 copy-start.1
  5.6 0.9 copy-done.1
  6.5 120.7 %shard_map.93 = (f32[64,256]{1,0:T(8,128)S(1)}, f32[64,384]{1,0:T(8,128)S(1)}, f32[3,64,64]{2,1,0:T(8,128)S(1)}, f32[3,64,64]{2,1,0:T(8,128)S(1)}) custom-call(s32[220]{0:T(256)S(1)} %concatenate.3.index_ref, bf16[32,128,128]{2,1,0:T(8,128)(2,1)S(1)} %bitcast.12, s32[8,256]{1,0:T(8,128)S(1)} %reshape.124.user_degree_ref, ...), custom_call_target="tpu_custom_call" | custom-call | tf_op jit(solution)/shard_map/pallas_call | solution.py:539
  127.2 0.6 copy.15
  127.8 0.6 copy.16
  128.4 0.6 copy.17
  129.1 0.6 copy.18
  (8 shorter events, 0.1 us)
Async XLA Ops:
  1.3 0.7 copy-start.4
  3.0 0.7 copy-start.2
  3.7 0.7 copy-start.3
  4.4 1.2 copy-start
  5.6 0.9 copy-start.1

commit v3 on v2

--- a/solution.py
+++ b/solution.py
@@ -175,14 +175,15 @@
     row_blocks,
     col_blocks,
     index_ref,
-    tiles_ref,
+    tiles_hbm,
     user_degree_ref,
     item_degree_ref,
-    start_ref,
+    start_hbm,
     left_ref,
     right_ref,
     left_factor_ref,
     right_factor_ref,
+    tiles_ref,
     item_all,
     user_all,
     split,
@@ -200,10 +201,14 @@
     gram_row,
     gram_sum,
     gram_col,
+    gram_all,
+    s_in,
     s_gr,
     r_gr,
     s_gc,
     r_gc,
+    s_ga,
+    r_ga,
     s_ir,
     r_ir,
     s_uz,
@@ -225,12 +230,18 @@
     sibling = col + 1 - 2 * core
     slots = tiles_ref.shape[0]
     width = tiles_ref.shape[1]
-    block = start_ref.shape[0]
+    block = item_raw.shape[0]
     half = block // 2
-    user_group = user_all.shape[2]
-    item_group = item_all.shape[2]
+    part = half // n_row
+    user_group = user_all.shape[3]
+    item_group = item_all.shape[3]
     user_per = user_group // width
     item_per = item_group // width
+
+    start_in = pltpu.make_async_copy(start_hbm, item_raw, s_in.at[0])
+    start_in.start()
+    tiles_in = pltpu.make_async_copy(tiles_hbm, tiles_ref, s_in.at[1])
+    tiles_in.start()
 
     barrier = pltpu.get_barrier_semaphore()
     for d in range(1, n_row):
@@ -241,7 +252,6 @@
         pl.semaphore_signal(
             barrier, inc=1, device_id=(row, lax.rem(col + d, n_col)), device_id_type=MESH
         )
-    pl.semaphore_wait(barrier, n_row + n_col - 2)
 
     def send(src, dst, s_sem, r_sem, target):
         copy = pltpu.make_async_remote_copy(
@@ -260,27 +270,28 @@
 
     def gram_start(raw, way):
         gram = dot_high(raw, raw, NT)
-        gram_own[way] = jnp.concatenate([gram[:half], gram[half:]], axis=1)
+        packed = jnp.concatenate([gram[:half], gram[half:]], axis=1)
+        for i in range(n_row):
+            gram_own[way, i] = packed[i * part : (i + 1) * part]
         copies = []
         for d in range(1, n_row):
+            target = lax.rem(row + d, n_row)
             copies.append(
                 send(
-                    gram_own.at[way],
+                    gram_own.at[way, target],
                     gram_row.at[way, d],
                     s_gr.at[way, d],
                     r_gr.at[way, d],
-                    (lax.rem(row + d, n_row), col),
+                    (target, col),
                 )
             )
         return copies
 
     def gram_middle(copies, way):
-        gram_row[way, 0] = gram_own[way]
-        for copy in copies:
-            copy.wait_recv()
-        total = gram_row[way, row]
-        for i in range(1, n_row):
-            total = total + gram_row[way, lax.rem(row - i + n_row, n_row)]
+        total = gram_own[way, row]
+        for d in range(1, n_row):
+            copies[d - 1].wait_recv()
+            total = total + gram_row[way, d]
         gram_sum[way] = total
         out = []
         for d in range(1, n_col):
@@ -295,195 +306,254 @@
             )
         return out
 
+    def gram_late(copies, way):
+        for copy in copies:
+            copy.wait_recv()
+        gram_col[way, 0] = gram_sum[way]
+        total = gram_col[way, col]
+        for j in range(1, n_col):
+            total = total + gram_col[way, lax.rem(col - j + n_col, n_col)]
+        gram_all[way, row] = total
+        out = []
+        for d in range(1, n_row):
+            out.append(
+                send(
+                    gram_all.at[way, row],
+                    gram_all.at[way, row],
+                    s_ga.at[way, d],
+                    r_ga.at[way, d],
+                    (lax.rem(row + d, n_row), col),
+                )
+            )
+        return out
+
     def gram_end(copies, way):
         for copy in copies:
             copy.wait_recv()
-        total = jnp.zeros((half, 2 * block), jnp.float32)
-        gram_col[way, 0] = gram_sum[way]
-        for j in range(n_col):
-            total = total + gram_col[way, lax.rem(col - j + n_col, n_col)]
+        total = jnp.concatenate([gram_all[way, i] for i in range(n_row)], axis=0)
         gram = jnp.concatenate([total[:, :block], total[:, block:]], axis=0)
         return factor_and_inverse(gram)
 
-    def put_split(first_block, values):
+    def put_split(h, first_block, values):
         for b in range(values.shape[1] // width):
-            part = values[:, b * width : (b + 1) * width]
-            high = part.astype(jnp.bfloat16)
-            low = (part - high.astype(jnp.float32)).astype(jnp.bfloat16)
-            split[first_block + b] = jnp.concatenate([high, low], axis=0)
-
-    def products(base, dims):
+            piece = values[:, b * width : (b + 1) * width]
+            high = piece.astype(jnp.bfloat16)
+            low = (piece - high.astype(jnp.float32)).astype(jnp.bfloat16)
+            split[h, first_block + b] = jnp.concatenate([high, low], axis=0)
+
+    def products(h, base, dims):
         def one(t, total):
             tile = tiles_ref[index_ref[base + t]]
-            vectors = split[index_ref[base + slots + t]]
+            vectors = split[h, index_ref[base + slots + t]]
             keep = index_ref[base + 2 * slots + t].astype(jnp.float32)
             both = lax.dot_general(
                 vectors, tile, dims, preferred_element_type=jnp.float32
             )
-            total = total * keep + (both[:block] + both[block:])
-            running[t] = total
+            total = total * keep + (both[:half] + both[half:])
+            running[h, t] = total
             return total
 
-        lax.fori_loop(
-            0, slots, one, jnp.zeros((block, width), jnp.float32), unroll=8
-        )
-
-    running[slots] = jnp.zeros((block, width), jnp.float32)
+        lax.fori_loop(0, slots, one, jnp.zeros((half, width), jnp.float32), unroll=8)
+
     forward_base = 0
     forward_last = 3 * slots
     backward_base = forward_last + row_blocks
     backward_last = backward_base + 3 * slots
 
-    item_raw[...] = start_ref[...]
+    for h in range(2):
+        running[h, slots] = jnp.zeros((half, width), jnp.float32)
     user_basis[...] = jnp.zeros_like(user_basis)
+    start_in.wait()
+    pl.semaphore_wait(barrier, n_row + n_col - 2)
+    tiles_in.wait()
 
     def step(k, carry):
         raw = item_raw[...]
         scaled = raw * item_scale
-        item_all[row] = scaled
-        moved = []
-        for d in range(1, n_row):
-            moved.append(
-                send(
-                    item_all.at[row],
-                    item_all.at[row],
-                    s_ir.at[d],
-                    r_ir.at[d],
-                    (lax.rem(row + d, n_row), col),
-                )
-            )
+        moved = [[], []]
+
+        def send_items(h):
+            item_all[h, row] = scaled[h * half : (h + 1) * half]
+            for d in range(1, n_row):
+                moved[h].append(
+                    send(
+                        item_all.at[h, row],
+                        item_all.at[h, row],
+                        s_ir.at[h, d],
+                        r_ir.at[h, d],
+                        (lax.rem(row + d, n_row), col),
+                    )
+                )
+
+        def take_items(h):
+            for d in range(1, n_row):
+                moved[h][d - 1].wait_recv()
+                source = lax.rem(row - d + n_row, n_row)
+                put_split(h, source * item_per, item_all[h, source])
+
+        pair = [[], []]
+        across = [[], []]
+
+        def send_pair(h):
+            for core_at in range(2):
+                for z_at in range(n_z):
+                    for b in range(user_per):
+                        owned = (z_at * 2 + core_at) * user_per + b
+                        user_send[
+                            h, core_at * n_z + z_at, :, b * width : (b + 1) * width
+                        ] = running[h, index_ref[forward_last + owned]]
+            for d in list(range(1, n_z)) + [0]:
+                target_z = lax.rem(z + d, n_z)
+                pair[h].append(
+                    send(
+                        user_send.at[h, (1 - core) * n_z + target_z],
+                        sibling_in.at[h, target_z],
+                        s_sib.at[h, d],
+                        r_sib.at[h, d],
+                        (row, sibling),
+                    )
+                )
+
+        def send_across(h):
+            for d in range(1, n_z):
+                target_z = lax.rem(z + d, n_z)
+                pair[h][d - 1].wait_recv()
+                user_send2[h, target_z] = (
+                    user_send[h, core * n_z + target_z] + sibling_in[h, target_z]
+                )
+                across[h].append(
+                    send(
+                        user_send2.at[h, target_z],
+                        user_in.at[h, z],
+                        s_z.at[h, d],
+                        r_z.at[h, d],
+                        (row, target_z * 2 + core),
+                    )
+                )
+            pair[h][n_z - 1].wait_recv()
+            return user_send[h, core * n_z + z] + sibling_in[h, z]
+
+        send_items(0)
         sent = gram_start(raw, 0)
-        put_split(row * item_per, scaled)
-        for d in range(1, n_row):
-            moved[d - 1].wait_recv()
-            source = lax.rem(row - d + n_row, n_row)
-            put_split(source * item_per, item_all[source])
+        send_items(1)
+        for h in range(2):
+            put_split(h, row * item_per, scaled[h * half : (h + 1) * half])
+        take_items(0)
         sent2 = gram_middle(sent, 0)
-        products(forward_base, NT)
-        pair = []
-        for core_at in range(2):
-            for z_at in range(n_z):
-                for b in range(user_per):
-                    user_send[core_at * n_z + z_at, :, b * width : (b + 1) * width] = (
-                        running[
-                            index_ref[
-                                forward_last + (z_at * 2 + core_at) * user_per + b
-                            ]
-                        ]
-                    )
-        for d in list(range(1, n_z)) + [0]:
-            target_z = lax.rem(z + d, n_z)
-            pair.append(
-                send(
-                    user_send.at[(1 - core) * n_z + target_z],
-                    sibling_in.at[target_z],
-                    s_sib.at[d],
-                    r_sib.at[d],
-                    (row, sibling),
-                )
-            )
-        across = []
-        for d in range(1, n_z):
-            target_z = lax.rem(z + d, n_z)
-            pair[d - 1].wait_recv()
-            user_send2[target_z] = (
-                user_send[core * n_z + target_z] + sibling_in[target_z]
-            )
-            across.append(
-                send(
-                    user_send2.at[target_z],
-                    user_in.at[z],
-                    s_z.at[d],
-                    r_z.at[d],
-                    (row, target_z * 2 + core),
-                )
-            )
-        pair[n_z - 1].wait_recv()
-        summed = user_send[core * n_z + z] + sibling_in[z]
-        factor_t, inverse = gram_end(sent2, 0)
+        products(0, forward_base, NT)
+        send_pair(0)
+        take_items(1)
+        summed0 = send_across(0)
+        products(1, forward_base, NT)
+        send_pair(1)
+        sent3 = gram_late(sent2, 0)
+        summed1 = send_across(1)
+        factor_t, inverse = gram_end(sent3, 0)
         right_factor_ref[lax.rem(k + STEPS - 1, STEPS)] = factor_t.T
         item_basis[...] = dot_high(inverse, raw)
         correction = dot_high(factor_t, user_basis[...])
-        for d in range(1, n_z):
-            across[d - 1].wait_recv()
-            summed = summed + user_in[lax.rem(z - d + n_z, n_z)]
+        sums = [summed0, summed1]
+        for h in range(2):
+            for d in range(1, n_z):
+                across[h][d - 1].wait_recv()
+                sums[h] = sums[h] + user_in[h, lax.rem(z - d + n_z, n_z)]
+        summed = jnp.concatenate(sums, axis=0)
         forward = dot_high(inverse, summed * user_scale) - correction
-        for copy in sent + sent2 + moved + pair + across:
-            copy.wait_send()
+        for group in [sent, sent2, sent3] + moved + pair + across:
+            for copy in group:
+                copy.wait_send()
 
         scaled = forward * user_scale
-        user_all[col] = scaled
-        moved = []
-        for d in range(1, n_z):
-            moved.append(
+        moved_u = [[], []]
+        passed = [[], []]
+
+        def send_users(h):
+            user_all[h, col] = scaled[h * half : (h + 1) * half]
+            for d in range(1, n_z):
+                moved_u[h].append(
+                    send(
+                        user_all.at[h, col],
+                        user_all.at[h, col],
+                        s_uz.at[h, d],
+                        r_uz.at[h, d],
+                        (row, lax.rem(z + d, n_z) * 2 + core),
+                    )
+                )
+            pass_on(h, col, 0)
+
+        def pass_on(h, source, d):
+            passed[h].append(
                 send(
-                    user_all.at[col],
-                    user_all.at[col],
-                    s_uz.at[d],
-                    r_uz.at[d],
-                    (row, lax.rem(z + d, n_z) * 2 + core),
+                    user_all.at[h, source],
+                    user_all.at[h, source],
+                    s_us.at[h, d],
+                    r_us.at[h, d],
+                    (row, sibling),
                 )
             )
-        passed = [
-            send(
-                user_all.at[col],
-                user_all.at[col],
-                s_us.at[0],
-                r_us.at[0],
-                (row, sibling),
-            )
-        ]
+
+        def take_users(h):
+            passed[h][0].wait_recv()
+            put_split(h, sibling * user_per, user_all[h, sibling])
+            for d in range(1, n_z):
+                moved_u[h][d - 1].wait_recv()
+                source = lax.rem(z - d + n_z, n_z) * 2 + core
+                pass_on(h, source, d)
+                put_split(h, source * user_per, user_all[h, source])
+            for d in range(1, n_z):
+                passed[h][d].wait_recv()
+                source = lax.rem(z - d + n_z, n_z) * 2 + 1 - core
+                put_split(h, source * user_per, user_all[h, source])
+
+        back = [[], []]
+
+        def send_rows(h):
+            for j in range(n_row):
+                for b in range(item_per):
+                    item_send[h, j, :, b * width : (b + 1) * width] = running[
+                        h, index_ref[backward_last + j * item_per + b]
+                    ]
+            for d in range(1, n_row):
+                target = lax.rem(row + d, n_row)
+                back[h].append(
+                    send(
+                        item_send.at[h, target],
+                        item_in.at[h, row],
+                        s_row.at[h, d],
+                        r_row.at[h, d],
+                        (target, col),
+                    )
+                )
+
+        send_users(0)
         sent = gram_start(forward, 1)
-        put_split(col * user_per, scaled)
+        send_users(1)
+        for h in range(2):
+            put_split(h, col * user_per, scaled[h * half : (h + 1) * half])
         sent2 = gram_middle(sent, 1)
-        passed[0].wait_recv()
-        put_split(sibling * user_per, user_all[sibling])
-        for d in range(1, n_z):
-            moved[d - 1].wait_recv()
-            source = lax.rem(z - d + n_z, n_z) * 2 + core
-            passed.append(
-                send(
-                    user_all.at[source],
-                    user_all.at[source],
-                    s_us.at[d],
-                    r_us.at[d],
-                    (row, sibling),
-                )
-            )
-            put_split(source * user_per, user_all[source])
-        for d in range(1, n_z):
-            passed[d].wait_recv()
-            source = lax.rem(z - d + n_z, n_z) * 2 + 1 - core
-            put_split(source * user_per, user_all[source])
-        products(backward_base, NN)
-        for j in range(n_row):
-            for b in range(item_per):
-                item_send[j, :, b * width : (b + 1) * width] = running[
-                    index_ref[backward_last + j * item_per + b]
-                ]
-        across = []
-        for d in range(1, n_row):
-            target = lax.rem(row + d, n_row)
-            across.append(
-                send(
-                    item_send.at[target],
-                    item_in.at[row],
-                    s_row.at[d],
-                    r_row.at[d],
-                    (target, col),
-                )
-            )
-        factor_t, inverse = gram_end(sent2, 1)
+        take_users(0)
+        products(0, backward_base, NN)
+        send_rows(0)
+        sent3 = gram_late(sent2, 1)
+        take_users(1)
+        products(1, backward_base, NN)
+        send_rows(1)
+        factor_t, inverse = gram_end(sent3, 1)
         left_factor_ref[k] = factor_t.T
         user_basis[...] = dot_high(inverse, forward)
         correction = dot_high(factor_t, item_basis[...])
-        summed = item_send[row]
-        for d in range(1, n_row):
-            across[d - 1].wait_recv()
-            summed = summed + item_in[lax.rem(row - d + n_row, n_row)]
+        sums = []
+        for h in range(2):
+            total = item_send[h, row]
+            for d in range(1, n_row):
+                back[h][d - 1].wait_recv()
+                total = total + item_in[h, lax.rem(row - d + n_row, n_row)]
+            sums.append(total)
+        summed = jnp.concatenate(sums, axis=0)
         item_raw[...] = dot_high(inverse, summed * item_scale) - correction
-        for copy in sent + sent2 + moved + passed + across:
-            copy.wait_send()
+        for group in [sent, sent2, sent3] + moved_u + passed + back:
+            for copy in group:
+                copy.wait_send()
         return carry
 
     lax.fori_loop(0, STEPS, step, 0)
@@ -492,10 +562,11 @@
     sent = gram_start(raw, 0)
     left_ref[...] = user_basis[...] * math.sqrt(row_blocks * width * n_row)
     sent2 = gram_middle(sent, 0)
-    factor_t, inverse = gram_end(sent2, 0)
+    sent3 = gram_late(sent2, 0)
+    factor_t, inverse = gram_end(sent3, 0)
     right_factor_ref[STEPS - 1] = factor_t.T
     right_ref[...] = dot_high(inverse, raw) * math.sqrt(col_blocks * width * n_col)
-    for copy in sent + sent2:
+    for copy in sent + sent2 + sent3:
         copy.wait_send()
 
 
@@ -536,6 +607,9 @@
     f32 = jnp.float32
     dma = pltpu.SemaphoreType.DMA
     n_z = n_col // 2
+    half = block // 2
+    part = half // n_row
+    anywhere = pl.BlockSpec(memory_space=pl.ANY)
     out = pl.pallas_call(
         functools.partial(kernel, n_row, n_col, row_blocks, col_blocks),
         out_shape=(
@@ -544,42 +618,47 @@
             jax.ShapeDtypeStruct((STEPS, block, block), f32),
             jax.ShapeDtypeStruct((STEPS, block, block), f32),
         ),
-        in_specs=[pl.BlockSpec(memory_space=pltpu.SMEM)] + [vmem] * 4,
+        in_specs=[pl.BlockSpec(memory_space=pltpu.SMEM), anywhere, vmem, vmem, anywhere],
         out_specs=(vmem,) * 4,
         scratch_shapes=[
-            pltpu.VMEM((n_row, block, item_group), f32),
-            pltpu.VMEM((n_col, block, user_group), f32),
-            pltpu.VMEM((max(row_blocks, col_blocks), 2 * block, width), jnp.bfloat16),
-            pltpu.VMEM((slots + 1, block, width), f32),
-            pltpu.VMEM((n_col, block, user_group), f32),
-            pltpu.VMEM((n_z, block, user_group), f32),
-            pltpu.VMEM((n_z, block, user_group), f32),
-            pltpu.VMEM((n_z, block, user_group), f32),
-            pltpu.VMEM((n_row, block, item_group), f32),
-            pltpu.VMEM((n_row, block, item_group), f32),
+            pltpu.VMEM((slots, width, width), tiles.dtype),
+            pltpu.VMEM((2, n_row, half, item_group), f32),
+            pltpu.VMEM((2, n_col, half, user_group), f32),
+            pltpu.VMEM((2, max(row_blocks, col_blocks), block, width), jnp.bfloat16),
+            pltpu.VMEM((2, slots + 1, half, width), f32),
+            pltpu.VMEM((2, n_col, half, user_group), f32),
+            pltpu.VMEM((2, n_z, half, user_group), f32),
+            pltpu.VMEM((2, n_z, half, user_group), f32),
+            pltpu.VMEM((2, n_z, half, user_group), f32),
+            pltpu.VMEM((2, n_row, half, item_group), f32),
+            pltpu.VMEM((2, n_row, half, item_group), f32),
             pltpu.VMEM((block, item_group), f32),
             pltpu.VMEM((block, item_group), f32),
             pltpu.VMEM((block, user_group), f32),
-            pltpu.VMEM((2, block // 2, 2 * block), f32),
-            pltpu.VMEM((2, n_row, block // 2, 2 * block), f32),
-            pltpu.VMEM((2, block // 2, 2 * block), f32),
-            pltpu.VMEM((2, n_col, block // 2, 2 * block), f32),
+            pltpu.VMEM((2, n_row, part, 2 * block), f32),
+            pltpu.VMEM((2, n_row, part, 2 * block), f32),
+            pltpu.VMEM((2, part, 2 * block), f32),
+            pltpu.VMEM((2, n_col, part, 2 * block), f32),
+            pltpu.VMEM((2, n_row, part, 2 * block), f32),
+            dma((2,)),
             dma((2, n_row)),
             dma((2, n_row)),
             dma((2, n_col)),
             dma((2, n_col)),
-            dma((n_row,)),
-            dma((n_row,)),
-            dma((n_z,)),
-            dma((n_z,)),
-            dma((n_z,)),
-            dma((n_z,)),
-            dma((n_z,)),
-            dma((n_z,)),
-            dma((n_z,)),
-            dma((n_z,)),
-            dma((n_row,)),
-            dma((n_row,)),
+            dma((2, n_row)),
+            dma((2, n_row)),
+            dma((2, n_row)),
+            dma((2, n_row)),
+            dma((2, n_z)),
+            dma((2, n_z)),
+            dma((2, n_z)),
+            dma((2, n_z)),
+            dma((2, n_z)),
+            dma((2, n_z)),
+            dma((2, n_z)),
+            dma((2, n_z)),
+            dma((2, n_row)),
+            dma((2, n_row)),
         ],
         compiler_params=pltpu.CompilerParams(
             collective_id=0, has_side_effects=True, vmem_limit_bytes=32 * 1024 * 1024
@@ -609,7 +688,8 @@
         cells = mesh.shape["row"] * mesh.shape["col"]
         owned = (args[3].shape[0] // cells, args[4].shape[0] // cells)
         form = per_device
-        if owned[0] % tile_width or owned[1] % tile_width:
+        sliver = (args[5].shape[0] // 2) % (8 * mesh.shape["row"])
+        if owned[0] % tile_width or owned[1] % tile_width or sliver:
             form = per_device_arrays
         return jax.shard_map(
             form, mesh=mesh, in_specs=in_specs, out_specs=out_specs, check_vma=False

time: 130 us -> 122 us (0.938)
  Pallas kernels: 121 us -> 113 us
    pallas_call x1, Pallas kernels: 121 us -> 113 us  [per_device(): pl.pallas_call(functools.partial(kernel, n_row, n_col, row_blocks, col_bl...]
where the time goes in v3:
time: 122 us
  Pallas kernels  113 us (93%)
  local copies, waits for them, and re-layouts  6.7 us (5%)
  between operations  1.34 us (1%)
    pallas_call x1, Pallas kernels, per_device(): pl.pallas_call(functools.partial(kernel, n_row, n_col, row_blocks, col_bl...  113 us
    unnamed x14, local copies, waits for them, and re-layouts  6.61 us

profile of v3, /device:TPU:0, one launch (start us, length us, event | category | flops | bytes accessed | tf_op | source)
XLA Modules:
  0.0 122.0 jit_solution(2727413402351743138)
XLA Ops:
  1.3 0.0 copy-start.4
  1.3 0.6 copy-done.4
  2.0 0.2 convert_reduce_fusion.1
  2.1 0.2 convert_reduce_fusion
  2.3 0.1 select_reduce_fusion.6
  2.5 0.1 select_reduce_fusion.7
  2.6 0.2 fusion.3
  2.8 0.2 select_reduce_fusion
  3.0 0.0 copy-start.2
  3.0 0.1 concatenate.3.index_ref
  3.1 0.6 copy-done.2
  3.7 0.0 copy-start.3
  3.7 0.7 copy-done.3
  4.4 0.0 copy-start
  4.4 1.2 %copy-done = bf16[1,1,32,128,128]{4,3,2,1,0:T(8,128)(2,1)S(1)} copy-done((bf16[1,1,32,128,128]{4,3,2,1,0:T(8,128)(2,1)S(1)}, bf16[1,1,32,128,128]{4,3,2,1,0:T(8,128)(2,1)}, u32[]{:S(2)}) %copy-start) | copy-done | bytes 1048600
  5.6 0.0 copy-start.1
  5.6 0.9 copy-done.1
  6.5 112.9 %shard_map.93 = (f32[64,256]{1,0:T(8,128)S(1)}, f32[64,384]{1,0:T(8,128)S(1)}, f32[3,64,64]{2,1,0:T(8,128)S(1)}, f32[3,64,64]{2,1,0:T(8,128)S(1)}) custom-call(s32[220]{0:T(256)S(1)} %concatenate.3.index_ref, bf16[32,128,128]{2,1,0:T(8,128)(2,1)S(1)} %bitcast.12, s32[8,256]{1,0:T(8,128)S(1)} %reshape.124.user_degree_ref, ...), custom_call_target="tpu_custom_call" | custom-call | tf_op jit(solution)/shard_map/pallas_call | solution.py:613
  119.4 0.6 copy.15
  120.1 0.6 copy.16
  120.7 0.6 copy.17
  121.3 0.6 copy.18
  (8 shorter events, 0.1 us)
Async XLA Ops:
  1.3 0.7 copy-start.4
  3.0 0.7 copy-start.2
  3.7 0.7 copy-start.3
  4.4 1.2 %copy-start = (bf16[1,1,32,128,128]{4,3,2,1,0:T(8,128)(2,1)S(1)}, bf16[1,1,32,128,128]{4,3,2,1,0:T(8,128)(2,1)}, u32[]{:S(2)}) copy-start(bf16[1,1,32,128,128]{4,3,2,1,0:T(8,128)(2,1)} %param.6) | copy-start | bytes 3145732
  5.6 0.9 copy-start.1

commit v4 on v3

--- a/solution.py
+++ b/solution.py
@@ -353,7 +353,7 @@
             running[h, t] = total
             return total
 
-        lax.fori_loop(0, slots, one, jnp.zeros((half, width), jnp.float32), unroll=8)
+        lax.fori_loop(0, slots, one, jnp.zeros((half, width), jnp.float32), unroll=16)
 
     forward_base = 0
     forward_last = 3 * slots
@@ -402,22 +402,20 @@
                         user_send[
                             h, core_at * n_z + z_at, :, b * width : (b + 1) * width
                         ] = running[h, index_ref[forward_last + owned]]
-            for d in list(range(1, n_z)) + [0]:
-                target_z = lax.rem(z + d, n_z)
-                pair[h].append(
-                    send(
-                        user_send.at[h, (1 - core) * n_z + target_z],
-                        sibling_in.at[h, target_z],
-                        s_sib.at[h, d],
-                        r_sib.at[h, d],
-                        (row, sibling),
-                    )
-                )
+            pair[h].append(
+                send(
+                    user_send.at[h, pl.ds((1 - core) * n_z, n_z)],
+                    sibling_in.at[h],
+                    s_sib.at[h],
+                    r_sib.at[h],
+                    (row, sibling),
+                )
+            )
 
         def send_across(h):
+            pair[h][0].wait_recv()
             for d in range(1, n_z):
                 target_z = lax.rem(z + d, n_z)
-                pair[h][d - 1].wait_recv()
                 user_send2[h, target_z] = (
                     user_send[h, core * n_z + target_z] + sibling_in[h, target_z]
                 )
@@ -430,7 +428,6 @@
                         (row, target_z * 2 + core),
                     )
                 )
-            pair[h][n_z - 1].wait_recv()
             return user_send[h, core * n_z + z] + sibling_in[h, z]
 
         send_items(0)
@@ -452,6 +449,9 @@
         right_factor_ref[lax.rem(k + STEPS - 1, STEPS)] = factor_t.T
         item_basis[...] = dot_high(inverse, raw)
         correction = dot_high(factor_t, user_basis[...])
+        for group in [sent, sent2, sent3] + moved + pair:
+            for copy in group:
+                copy.wait_send()
         sums = [summed0, summed1]
         for h in range(2):
             for d in range(1, n_z):
@@ -459,9 +459,6 @@
                 sums[h] = sums[h] + user_in[h, lax.rem(z - d + n_z, n_z)]
         summed = jnp.concatenate(sums, axis=0)
         forward = dot_high(inverse, summed * user_scale) - correction
-        for group in [sent, sent2, sent3] + moved + pair + across:
-            for copy in group:
-                copy.wait_send()
 
         scaled = forward * user_scale
         moved_u = [[], []]
@@ -528,6 +525,8 @@
         send_users(0)
         sent = gram_start(forward, 1)
         send_users(1)
+        for copy in across[0] + across[1]:
+            copy.wait_send()
         for h in range(2):
             put_split(h, col * user_per, scaled[h * half : (h + 1) * half])
         sent2 = gram_middle(sent, 1)
@@ -542,6 +541,9 @@
         left_factor_ref[k] = factor_t.T
         user_basis[...] = dot_high(inverse, forward)
         correction = dot_high(factor_t, item_basis[...])
+        for group in [sent, sent2, sent3] + moved_u + passed:
+            for copy in group:
+                copy.wait_send()
         sums = []
         for h in range(2):
             total = item_send[h, row]
@@ -551,9 +553,8 @@
             sums.append(total)
         summed = jnp.concatenate(sums, axis=0)
         item_raw[...] = dot_high(inverse, summed * item_scale) - correction
-        for group in [sent, sent2, sent3] + moved_u + passed + back:
-            for copy in group:
-                copy.wait_send()
+        for copy in back[0] + back[1]:
+            copy.wait_send()
         return carry
 
     lax.fori_loop(0, STEPS, step, 0)
@@ -653,15 +654,15 @@
             dma((2, n_z)),
             dma((2, n_z)),
             dma((2, n_z)),
+            dma((2,)),
+            dma((2,)),
             dma((2, n_z)),
             dma((2, n_z)),
-            dma((2, n_z)),
-            dma((2, n_z)),
             dma((2, n_row)),
             dma((2, n_row)),
         ],
         compiler_params=pltpu.CompilerParams(
-            collective_id=0, has_side_effects=True, vmem_limit_bytes=32 * 1024 * 1024
+            collective_id=0, has_side_effects=True, vmem_limit_bytes=63 * 1024 * 1024
         ),
     )(
         index,

time: 122 us -> 122 us (level)
    unnamed x14 -> x16, local copies, waits for them, and re-layouts: 6.61 us -> 4.79 us
where the time goes in v4:
time: 122 us; the launch traced here: 121 us
  Pallas kernels  112 us (92%)
  local copies, waits for them, and re-layouts  6.64 us (5%)
  between operations  1.35 us (1%)
    pallas_call x1, Pallas kernels, per_device(): pl.pallas_call(functools.partial(kernel, n_row, n_col, row_blocks, col_bl...  112 us
    unnamed x16, local copies, waits for them, and re-layouts  4.79 us

profile of v4, /device:TPU:0, one launch (start us, length us, event | category | flops | bytes accessed | tf_op | source)
XLA Modules:
  0.0 121.4 jit_solution(2207330212545211870)
XLA Ops:
  1.3 0.0 copy-start.5
  1.3 0.6 copy-done.5
  2.0 0.2 convert_reduce_fusion.1
  2.1 0.2 convert_reduce_fusion
  2.3 0.1 select_reduce_fusion.6
  2.5 0.1 select_reduce_fusion.7
  2.6 0.2 fusion.3
  2.8 0.2 select_reduce_fusion
  3.0 0.0 copy-start.3
  3.0 0.7 concatenate.3.index_ref
  3.6 0.0 copy-done.3
  3.7 0.0 copy-start.4
  3.7 0.6 reshape.125.item_degree_ref
  4.3 0.1 copy-done.4
  4.4 0.6 reshape.124.user_degree_ref
  5.0 112.4 %shard_map.93 = (f32[64,256]{1,0:T(8,128)}, f32[64,384]{1,0:T(8,128)}, f32[3,64,64]{2,1,0:T(8,128)}, f32[3,64,64]{2,1,0:T(8,128)}) custom-call(s32[220]{0:T(256)} %concatenate.3.index_ref, bf16[32,128,128]{2,1,0:T(8,128)(2,1)} %bitcast.12, s32[8,256]{1,0:T(8,128)} %reshape.124.user_degree_ref, s32[4,384]{1,0:T(4,128)} %reshape.125.item_degree_ref, ...), custom_call_target="tpu_custom_call" | custom-call | tf_op jit(solution)/shard_map/pallas_call | solution.py:614
  117.4 0.0 copy-start.2
  117.4 1.5 %copy.15 = f32[64,256]{1,0:T(8,128)} copy(f32[64,256]{1,0:T(8,128)} %get-tuple-element.25) | data formatting | bytes 131072
  118.9 0.0 copy-done.2
  118.9 0.6 copy.16
  119.5 0.3 copy-done.1
  119.8 0.6 copy.17
  120.5 0.3 copy-done
  120.8 0.6 copy.18
  (8 shorter events, 0.0 us)
Async XLA Ops:
  1.3 0.7 copy-start.5
  3.0 0.7 copy-start.3
  3.7 0.7 copy-start.4
  117.4 1.5 %copy-start.2 = (f32[64,384]{1,0:T(8,128)S(1)}, f32[64,384]{1,0:T(8,128)}, u32[]{:S(2)}) copy-start(f32[64,384]{1,0:T(8,128)} %get-tuple-element.26) | copy-start | bytes 294916
  118.9 0.9 copy-start.1
  119.8 0.9 copy-start
